TPU v7x, 512 devices: a whole 4x4x16 slice. The times are simulated.
512 devices in a mesh: space: 64 (over x, z_hi, y, core), vel: 8 (over z_lo).
Axes of the slice: x: 4, y: 4, z: 16 (z_hi: 2, z_lo: 8; z = z_hi * 8 + z_lo), core: 2. Of those that a mesh axis runs over, the one named last changes fastest.
Arguments:
- density: float32 [128, 16, 4, 4096], P('space', None, None, 'vel'), may hold values from 0.2 to 2
- gain_left: float32 [4, 4096], replicated, may hold values from -4 to 4
- gain_right: float32 [4, 4096], replicated, may hold values from -4 to 4
- loss_kernel: float32 [4096], replicated, may hold values from -4 to 4
Outputs:
- evolved: float32 [128, 16, 4, 4096], P('space', None, None, 'vel')
All inputs are finite; a program needn't handle non-finite values.
Results may differ from a plain program's by a relative error of at most 0.0003.
Values sent between devices are 32-bit elements; how exact they have to be, the bound alone decides.
A program may use at most 64 MiB of HBM per device.

v0:
```python
import math

import jax
import jax.numpy as jnp
from jax import lax
from jax.sharding import PartitionSpec as P

M = 16


courant = 1.0 / 6.0
time_step = 0.25
rate_scale = 0.25
highest = lax.Precision.HIGHEST


def with_halo(block, sides, width):
    for axis, dim in sides:
        count = lax.axis_size(axis)
        forward = [(i, i + 1) for i in range(count - 1)]
        forward.append((count - 1, 0))
        backward = [(target, source) for source, target in forward]
        low = lax.ppermute(
            lax.slice_in_dim(block, block.shape[dim] - width, None, axis=dim), axis, forward
        )
        high = lax.ppermute(lax.slice_in_dim(block, 0, width, axis=dim), axis, backward)
        block = jnp.concatenate([low, block, high], axis=dim)
    return block


def cut_along(value, dim, devices):
    shape = value.shape
    parts = value.reshape(*shape[:dim], devices, shape[dim] // devices, *shape[dim + 1 :])
    return jnp.moveaxis(parts, dim, 0)


def cut_rows(length, count):
    unit = 8 if length >= 8 * count else 1
    return [length // unit * k // count * unit for k in range(1, count)]


def joined_along(parts, dim):
    parts = jnp.moveaxis(parts, 0, dim)
    shape = parts.shape
    return parts.reshape(*shape[:dim], shape[dim] * shape[dim + 1], *shape[dim + 2 :])


def cut_exchange(value, axis, pieces, split_dim, concat_dim):
    parts = cut_along(value, split_dim, lax.axis_size(axis))
    widest = max(range(1, max(2, parts.ndim - 1)), key=lambda d: parts.shape[d])
    gathered = []
    for piece in jnp.split(parts, cut_rows(parts.shape[widest], pieces), axis=widest):
        if piece.size:
            gathered.append(lax.all_to_all(piece, axis, split_axis=0, concat_axis=0, tiled=True))
    return joined_along(jnp.concatenate(gathered, axis=widest), concat_dim)


def sent_to_all(value, axis):
    devices = lax.axis_size(axis)
    return lax.all_to_all(
        jnp.broadcast_to(value[None], (devices, *value.shape)), axis, 0, 0, tiled=True
    )


def of_everyone(value, axis):
    return sent_to_all(value, axis).sum(axis=0)


def minmod(lower_diff, upper_diff):
    smaller = jnp.minimum(jnp.abs(lower_diff), jnp.abs(upper_diff))
    return jnp.where(lower_diff * upper_diff > 0.0, jnp.sign(lower_diff) * smaller, 0.0)


def face_jump(back_two, back_one, middle, ahead_one, ahead_two, positive):
    d_back = middle - back_one
    d_ahead = ahead_one - middle
    d_far_back = back_one - back_two
    d_far_ahead = ahead_two - ahead_one
    right_up = middle + 0.5 * minmod(d_back, d_ahead)
    left_up = back_one + 0.5 * minmod(d_far_back, d_back)
    right_down = ahead_one - 0.5 * minmod(d_ahead, d_far_ahead)
    left_down = middle - 0.5 * minmod(d_back, d_ahead)
    return jnp.where(positive, right_up - left_up, right_down - left_down)


def rolled_jump(field_now, roll_axis, positive):
    return face_jump(
        jnp.roll(field_now, 2, roll_axis),
        jnp.roll(field_now, 1, roll_axis),
        field_now,
        jnp.roll(field_now, -1, roll_axis),
        jnp.roll(field_now, -2, roll_axis),
        positive,
    )


def velocity(counter, grid_side):
    return (2.0 * counter.astype(jnp.float32) + 1.0) / grid_side - 1.0


def advect(field_now, vel_x, vel_y, vel_z):
    padded = with_halo(field_now, (("space", 0),), 2)
    jump_x = face_jump(
        padded[:-4], padded[1:-3], padded[2:-2], padded[3:-1], padded[4:], vel_x > 0.0
    )
    jump_y = rolled_jump(field_now, 1, vel_y > 0.0)
    jump_z = rolled_jump(field_now, 2, vel_z > 0.0)
    return field_now - courant * (vel_x * jump_x + vel_y * jump_y + vel_z * jump_z)


def dft_tables(grid_side):
    counter = jnp.arange(grid_side, dtype=jnp.int32)
    phases = counter[:, None] * counter[None, :] % grid_side
    angles = phases.astype(jnp.float32) * (2.0 * math.pi / grid_side)
    pair_index = jnp.arange(grid_side * grid_side, dtype=jnp.int32)
    outer_index = pair_index // grid_side
    inner_index = pair_index % grid_side
    phases_two = (
        outer_index[:, None] * outer_index[None, :] + inner_index[:, None] * inner_index[None, :]
    ) % grid_side
    angles_two = phases_two.astype(jnp.float32) * (2.0 * math.pi / grid_side)
    return (jnp.cos(angles), jnp.sin(angles), jnp.cos(angles_two), jnp.sin(angles_two))


def along_first(matrix, operand):
    return jnp.einsum("ka,naj->nkj", matrix, operand, precision=highest)


def along_last(operand, matrix):
    return jnp.einsum("naj,jk->nak", operand, matrix, precision=highest)


def spectral_change(spectra_in, gain_left, gain_right, loss_kernel, tables):
    cos_one, sin_one, cos_two, sin_two = tables
    grid_side = spectra_in.shape[1]
    norm_scale = 1.0 / grid_side**3
    real_first = along_last(spectra_in, cos_two)
    imag_first = -along_last(spectra_in, sin_two)
    spec_real = along_first(cos_one, real_first) + along_first(sin_one, imag_first)
    spec_imag = along_first(cos_one, imag_first) - along_first(sin_one, real_first)

    def inverse(kernel_modes, with_imag):
        kernel_grid = kernel_modes.reshape(grid_side, -1)
        mod_real = kernel_grid * spec_real
        mod_imag = kernel_grid * spec_imag
        mid_real = along_first(cos_one, mod_real) - along_first(sin_one, mod_imag)
        mid_imag = along_first(cos_one, mod_imag) + along_first(sin_one, mod_real)
        out_real = (along_last(mid_real, cos_two) - along_last(mid_imag, sin_two)) * norm_scale
        if with_imag:
            return (
                out_real,
                (along_last(mid_real, sin_two) + along_last(mid_imag, cos_two)) * norm_scale,
            )
        return (out_real, out_real)

    gain = jnp.zeros(spectra_in.shape, jnp.float32)
    for term_index in range(gain_left.shape[0]):
        left_real, left_imag = inverse(gain_left[term_index], True)
        right_real, right_imag = inverse(gain_right[term_index], True)
        gain = gain + (left_real * right_real - left_imag * right_imag)
    loss_real, unused_part = inverse(loss_kernel, False)
    return gain - spectra_in * loss_real


def moment_table(vel_x, vel_y, vel_z):
    speed_sq = vel_x * vel_x + vel_y * vel_y + vel_z * vel_z
    return jnp.stack([jnp.ones_like(vel_x), vel_x, vel_y, vel_z, speed_sq])


def per_device(density, gain_left, gain_right, loss_kernel):
    plane_count, line_count, column_count, share_count = density.shape
    grid_side = M
    speeds_here = lax.axis_index("vel") * share_count + jnp.arange(share_count, dtype=jnp.int32)
    vel_z = velocity(speeds_here // (grid_side * grid_side), grid_side)
    vel_x = velocity(speeds_here // grid_side % grid_side, grid_side)
    vel_y = velocity(speeds_here % grid_side, grid_side)
    tables = dft_tables(grid_side)
    advected = advect(density, vel_x, vel_y, vel_z)
    stacked = advected.reshape(plane_count, line_count * column_count, share_count)
    regrouped = lax.all_to_all(stacked, "vel", split_axis=1, concat_axis=2, tiled=True)
    item_count, cells_here, whole_count = regrouped.shape
    spectra_in = regrouped.reshape(item_count * cells_here, grid_side, whole_count // grid_side)
    change_here = spectral_change(spectra_in, gain_left, gain_right, loss_kernel, tables).reshape(
        regrouped.shape
    )
    returned_change = cut_exchange(change_here, "vel", 2, 2, 1)
    change = returned_change.reshape(density.shape)
    share_table = moment_table(vel_x, vel_y, vel_z)
    local_totals = jnp.einsum("ks,pcs->kpc", share_table, stacked, precision=highest)
    totals = of_everyone(local_totals, "vel")
    totals = totals.reshape(5, plane_count, line_count, column_count)
    weight = (2.0 / grid_side) ** 3
    mass_total = totals[0] * weight
    mean_flow_first = totals[1] * weight / mass_total
    mean_flow_second = totals[2] * weight / mass_total
    mean_flow_third = totals[3] * weight / mass_total
    kinetic_content = totals[4] * weight / mass_total
    cell_heat_level = (
        kinetic_content
        - (
            mean_flow_first * mean_flow_first
            + mean_flow_second * mean_flow_second
            + mean_flow_third * mean_flow_third
        )
    ) / 3.0
    gaussian_variance = 2.0 * math.pi * cell_heat_level
    gaussian_prefactor = mass_total / (gaussian_variance * jnp.sqrt(gaussian_variance))
    relative_motion_squared = (
        (vel_x - mean_flow_first[..., None]) ** 2
        + (vel_y - mean_flow_second[..., None]) ** 2
        + (vel_z - mean_flow_third[..., None]) ** 2
    )
    equilibrium_profile = gaussian_prefactor[..., None] * jnp.exp(
        -relative_motion_squared / (2.0 * cell_heat_level[..., None])
    )
    rate = (rate_scale * mass_total)[..., None]
    relaxed = (advected + time_step * change + time_step * rate * equilibrium_profile) / (
        1.0 + time_step * rate
    )
    return advect(relaxed, vel_x, vel_y, vel_z)


def solution(mesh):
    in_specs = (P("space", None, None, "vel"), P(), P(), P())
    out_specs = P("space", None, None, "vel")
    return jax.shard_map(
        per_device, mesh=mesh, in_specs=in_specs, out_specs=out_specs, check_vma=False
    )
```

profile of v0, /device:TPU:32, one launch (start us, length us, event | category | flops | bytes accessed | tf_op | source)
XLA Modules:
  0.0 223.6 jit_solution(11499677735029231607)
XLA Ops:
  1.2 18.9 %collective-permute-start.1 = (f32[2,16,4,512]{3,0,2,1:T(2,128)S(1)}, f32[2,16,4,512]{3,0,2,1:T(2,128)S(1)}, u32[]{:S(2)}, u32[]{:S(2)}) collective-permute-start(f32[2,16,4,512]{3,0,2,1:T(2,128)S(1)} %copy.134), channel_id=1, source_target_pairs={{8,0},{16,8},{24,16},{32,24},{40,32},{48,40},{56,48},{64,56},{72,6... | collective-permute-start | bytes 786440 | tf_op jit(solution)/shard_map/ppermute | solution.py:26
  20.1 1.9 collective-permute-start
  22.7 9.7 %collective-permute-done.1 = f32[2,16,4,512]{3,0,2,1:T(2,128)S(1)} collective-permute-done((f32[2,16,4,512]{3,0,2,1:T(2,128)S(1)}, f32[2,16,4,512]{3,0,2,1:T(2,128)S(1)}, u32[]{:S(2)}, u32[]{:S(2)}) %collective-permute-start.1) | collective-permute-done | bytes 262176 | tf_op jit(solution)/shard_map/ppermute | solution.py:26
  32.4 18.8 %collective-permute-done = f32[2,16,4,512]{3,0,2,1:T(2,128)S(1)} collective-permute-done((f32[2,16,4,512]{3,0,2,1:T(2,128)S(1)}, f32[2,16,4,512]{3,0,2,1:T(2,128)S(1)}, u32[]{:S(2)}, u32[]{:S(2)}) %collective-permute-start) | collective-permute-done | bytes 262176 | tf_op jit(solution)/shard_map/ppermute | solution.py:23
  51.1 7.1 %multiply_subtract_fusion.1 = f32[2,16,4,512]{3,0,2,1:T(2,128)} fusion(f32[2,16,4,512]{3,0,2,1:T(2,128)S(1)} %copy.134, f32[2,16,2,512]{3,0,2,1:T(2,128)S(1)} %get-tuple-element.47, f32[2,16,2,512]{3,0,2,1:T(2,128)S(1)} %get-tuple-element.46, f32[2,16,1,512]{3,0,2,1:T(2,128)S(1)} %get-tuple-element.43, f32[2,16,3,512]{3,0,2,1:T(2,128)S(1)} %get-tuple-element.45, ...), kind=kLoop, calls=%fused_computation.251 | loop fusion | flops 8126464 | bytes 2891264 | tf_op jit(solution)/shard_map/sub | solution.py:108
  58.3 6.1 %all-to-all-start = ((f32[2,64,512]{2,0,1:T(2,128)}), f32[2,64,512]{2,0,1:T(2,128)S(1)}, u32[]{:S(2)}, u32[]{:S(2)}) async-start(f32[2,64,512]{2,0,1:T(2,128)} %bitcast), calls=%async_computation | async-start | bytes 524288 | tf_op jit(solution)/shard_map/all_to_all | solution.py:180
  67.1 9.7 %all-to-all-done = f32[2,64,512]{2,0,1:T(2,128)S(1)} async-done(((f32[2,64,512]{2,0,1:T(2,128)}), f32[2,64,512]{2,0,1:T(2,128)S(1)}, u32[]{:S(2)}, u32[]{:S(2)}) %all-to-all-start) | async-done | bytes 262176 | tf_op jit(solution)/shard_map/all_to_all | solution.py:180
  76.8 5.2 %all-to-all-start.3 = ((f32[8,1,640]{2,1,0:T(1,128)}), f32[8,1,640]{2,1,0:T(1,128)S(1)}, u32[]{:S(2)}, u32[]{:S(2)}) async-start(f32[8,1,640]{2,1,0:T(1,128)} %reshape.487), calls=%async_computation.3 | async-start | bytes 40960 | tf_op jit(solution)/shard_map/all_to_all | solution.py:60
  83.7 1.4 convolution_negate_fusion
  94.4 1.6 fusion.138
  107.8 1.8 fusion.148
  125.9 1.4 fusion.5
  129.7 1.4 fusion.13
  133.4 1.6 fusion.21
  138.7 1.4 fusion.53
  141.6 1.4 fusion.51
  143.0 1.4 fusion.49
  144.5 1.4 fusion.48
  145.9 1.7 fusion.46
  147.6 1.4 fusion.45
  149.1 1.4 fusion.43
  150.5 1.5 fusion.42
  153.0 9.9 %all-to-all-start.2 = ((f32[8,2,4,512]{3,2,1,0:T(4,128)}), f32[8,2,4,512]{3,2,1,0:T(4,128)S(1)}, u32[]{:S(2)}, u32[]{:S(2)}) async-start(f32[8,2,4,512]{3,2,1,0:T(4,128)} %get-tuple-element.33), calls=%async_computation.2 | async-start | bytes 262144 | tf_op jit(solution)/shard_map/all_to_all | solution.py:54
  164.3 8.2 %all-to-all-done.2 = f32[8,2,4,512]{3,2,1,0:T(4,128)S(1)} async-done(((f32[8,2,4,512]{3,2,1,0:T(4,128)}), f32[8,2,4,512]{3,2,1,0:T(4,128)S(1)}, u32[]{:S(2)}, u32[]{:S(2)}) %all-to-all-start.2) | async-done | bytes 131104 | tf_op jit(solution)/shard_map/all_to_all | solution.py:54
  172.5 5.1 %all-to-all-start.1 = ((f32[8,2,4,512]{3,2,1,0:T(4,128)}), f32[8,2,4,512]{3,2,1,0:T(4,128)S(1)}, u32[]{:S(2)}, u32[]{:S(2)}) async-start(f32[8,2,4,512]{3,2,1,0:T(4,128)} %get-tuple-element.32), calls=%async_computation.1 | async-start | bytes 262144 | tf_op jit(solution)/shard_map/all_to_all | solution.py:54
  179.5 7.7 %all-to-all-done.1 = f32[8,2,4,512]{3,2,1,0:T(4,128)S(1)} async-done(((f32[8,2,4,512]{3,2,1,0:T(4,128)}), f32[8,2,4,512]{3,2,1,0:T(4,128)S(1)}, u32[]{:S(2)}, u32[]{:S(2)}) %all-to-all-start.1) | async-done | bytes 131104 | tf_op jit(solution)/shard_map/all_to_all | solution.py:54
  187.5 1.7 add_divide_fusion
  189.6 1.9 collective-permute-start.3
  191.5 2.4 %collective-permute-start.2 = (f32[2,16,4,512]{3,0,2,1:T(2,128)S(1)}, f32[2,16,4,512]{3,0,2,1:T(2,128)S(1)}, u32[]{:S(2)}, u32[]{:S(2)}) collective-permute-start(f32[2,16,4,512]{3,0,2,1:T(2,128)S(1)} %add_divide_fusion), channel_id=1, source_target_pairs={{0,8},{8,16},{16,24},{24,32},{32,40},{40,48},{48,56},{56,64},{64,7... | collective-permute-start | bytes 786440 | tf_op jit(solution)/shard_map/ppermute | solution.py:23
  194.2 4.7 %collective-permute-done.3 = f32[2,16,4,512]{3,0,2,1:T(2,128)S(1)} collective-permute-done((f32[2,16,4,512]{3,0,2,1:T(2,128)S(1)}, f32[2,16,4,512]{3,0,2,1:T(2,128)S(1)}, u32[]{:S(2)}, u32[]{:S(2)}) %collective-permute-start.3) | collective-permute-done | bytes 262176 | tf_op jit(solution)/shard_map/ppermute | solution.py:26
  198.8 17.0 %collective-permute-done.2 = f32[2,16,4,512]{3,0,2,1:T(2,128)S(1)} collective-permute-done((f32[2,16,4,512]{3,0,2,1:T(2,128)S(1)}, f32[2,16,4,512]{3,0,2,1:T(2,128)S(1)}, u32[]{:S(2)}, u32[]{:S(2)}) %collective-permute-start.2) | collective-permute-done | bytes 262176 | tf_op jit(solution)/shard_map/ppermute | solution.py:23
  215.8 6.5 %multiply_subtract_fusion = f32[2,16,4,512]{3,0,2,1:T(2,128)S(1)} fusion(f32[2,16,4,512]{3,0,2,1:T(2,128)S(1)} %add_divide_fusion, f32[2,16,2,512]{3,0,2,1:T(2,128)S(1)} %get-tuple-element.31, f32[2,16,2,512]{3,0,2,1:T(2,128)S(1)} %get-tuple-element.30, f32[2,16,1,512]{3,0,2,1:T(2,128)S(1)} %get-tuple-element.27, ...), kind=kLoop, calls=%fused_computation.242 | loop fusion | flops 8126464 | bytes 2891264 | tf_op jit(solution)/shard_map/sub | solution.py:108
  (136 shorter events, 58.5 us)
Async XLA Ops:
  1.2 31.2 %collective-permute-start.1 = (f32[2,16,4,512]{3,0,2,1:T(2,128)S(1)}, f32[2,16,4,512]{3,0,2,1:T(2,128)S(1)}, u32[]{:S(2)}, u32[]{:S(2)}) collective-permute-start(f32[2,16,4,512]{3,0,2,1:T(2,128)S(1)} %copy.134), channel_id=1, source_target_pairs={{8,0},{16,8},{24,16},{32,24},{40,32},{48,40},{56,48},{64,56},{72,6... | collective-permute-start | bytes 786440 | tf_op jit(solution)/shard_map/ppermute | solution.py:26
  20.1 31.1 %collective-permute-start = (f32[2,16,4,512]{3,0,2,1:T(2,128)S(1)}, f32[2,16,4,512]{3,0,2,1:T(2,128)S(1)}, u32[]{:S(2)}, u32[]{:S(2)}) collective-permute-start(f32[2,16,4,512]{3,0,2,1:T(2,128)S(1)} %copy.134), channel_id=1, source_target_pairs={{0,8},{8,16},{16,24},{24,32},{32,40},{40,48},{48,56},{56,64},{64,7... | collective-permute-start | bytes 786440 | tf_op jit(solution)/shard_map/ppermute | solution.py:23
  58.3 6.1 %copy-start.2 = (f32[4096]{0:T(1024)S(1)}, f32[4096]{0:T(1024)}, u32[]{:S(2)}) copy-start(f32[4096]{0:T(1024)} %param.7) | copy-start | bytes 49156
  58.3 6.1 %copy-start = (f32[4,4096]{1,0:T(4,128)S(1)}, f32[4,4096]{1,0:T(4,128)}, u32[]{:S(2)}) copy-start(f32[4,4096]{1,0:T(4,128)} %param.6) | copy-start | bytes 196612
  58.3 6.1 %copy-start.1 = (f32[4,4096]{1,0:T(4,128)S(1)}, f32[4,4096]{1,0:T(4,128)}, u32[]{:S(2)}) copy-start(f32[4,4096]{1,0:T(4,128)} %param.5) | copy-start | bytes 196612
  58.3 18.5 %all-to-all-start = ((f32[2,64,512]{2,0,1:T(2,128)}), f32[2,64,512]{2,0,1:T(2,128)S(1)}, u32[]{:S(2)}, u32[]{:S(2)}) async-start(f32[2,64,512]{2,0,1:T(2,128)} %bitcast), calls=%async_computation | async-start | bytes 524288 | tf_op jit(solution)/shard_map/all_to_all | solution.py:180
  76.8 76.2 %all-to-all-start.3 = ((f32[8,1,640]{2,1,0:T(1,128)}), f32[8,1,640]{2,1,0:T(1,128)S(1)}, u32[]{:S(2)}, u32[]{:S(2)}) async-start(f32[8,1,640]{2,1,0:T(1,128)} %reshape.487), calls=%async_computation.3 | async-start | bytes 40960 | tf_op jit(solution)/shard_map/all_to_all | solution.py:60
  153.0 19.5 %all-to-all-start.2 = ((f32[8,2,4,512]{3,2,1,0:T(4,128)}), f32[8,2,4,512]{3,2,1,0:T(4,128)S(1)}, u32[]{:S(2)}, u32[]{:S(2)}) async-start(f32[8,2,4,512]{3,2,1,0:T(4,128)} %get-tuple-element.33), calls=%async_computation.2 | async-start | bytes 262144 | tf_op jit(solution)/shard_map/all_to_all | solution.py:54
  172.5 14.7 %all-to-all-start.1 = ((f32[8,2,4,512]{3,2,1,0:T(4,128)}), f32[8,2,4,512]{3,2,1,0:T(4,128)S(1)}, u32[]{:S(2)}, u32[]{:S(2)}) async-start(f32[8,2,4,512]{3,2,1,0:T(4,128)} %get-tuple-element.32), calls=%async_computation.1 | async-start | bytes 262144 | tf_op jit(solution)/shard_map/all_to_all | solution.py:54
  189.6 9.3 %collective-permute-start.3 = (f32[2,16,4,512]{3,0,2,1:T(2,128)S(1)}, f32[2,16,4,512]{3,0,2,1:T(2,128)S(1)}, u32[]{:S(2)}, u32[]{:S(2)}) collective-permute-start(f32[2,16,4,512]{3,0,2,1:T(2,128)S(1)} %add_divide_fusion), channel_id=1, source_target_pairs={{8,0},{16,8},{24,16},{32,24},{40,32},{48,40},{56,48},{64,56},{72,6... | collective-permute-start | bytes 786440 | tf_op jit(solution)/shard_map/ppermute | solution.py:26
  191.5 24.3 %collective-permute-start.2 = (f32[2,16,4,512]{3,0,2,1:T(2,128)S(1)}, f32[2,16,4,512]{3,0,2,1:T(2,128)S(1)}, u32[]{:S(2)}, u32[]{:S(2)}) collective-permute-start(f32[2,16,4,512]{3,0,2,1:T(2,128)S(1)} %add_divide_fusion), channel_id=1, source_target_pairs={{0,8},{8,16},{16,24},{24,32},{32,40},{40,48},{48,56},{56,64},{64,7... | collective-permute-start | bytes 786440 | tf_op jit(solution)/shard_map/ppermute | solution.py:23
where the time goes:
time: 228 us; the launch traced here: 224 us
  waiting for transfers between devices  75.7 us (33%)
  matrix products  70.5 us (31%)
  starting transfers between devices  51.5 us (23%)
  other arithmetic  16.3 us (7%)
  local copies, waits for them, and re-layouts  8.13 us (4%)
    dot_general x36, matrix products, along_last(): return jnp.einsum('naj,jk->nak', operand, matrix, precision=highest)  52.5 us
    ppermute x2, waiting for transfers between devices, with_halo(): lax.ppermute(lax.slice_in_dim(block, block.shape[dim] - width, None, axis...  35.8 us
    ppermute x2, starting transfers between devices, with_halo(): lax.ppermute(lax.slice_in_dim(block, 0, width, axis=dim), axis, backward)  20.8 us
    dot_general x40, matrix products, along_first(): return jnp.einsum('ka,naj->nkj', matrix, operand, precision=highest)  16.7 us
    all_to_all x2, waiting for transfers between devices, cut_exchange(): lax.all_to_all(piece, axis, split_axis=0, concat_axis=0, tiled=True)  15.9 us
    all_to_all x2, starting transfers between devices, cut_exchange(): lax.all_to_all(piece, axis, split_axis=0, concat_axis=0, tiled=True)  15 us
    ppermute x2, waiting for transfers between devices, with_halo(): lax.ppermute(lax.slice_in_dim(block, 0, width, axis=dim), axis, backward)  14.3 us
    sub x2, other arithmetic, advect(): field_now - courant * (vel_x * jump_x + vel_y * jump_y + vel_z * jump_z)  13.6 us
  transfers between devices with their start and end apart: 8, of which 7 were waited for; matrix products, arithmetic and copies ran while one was open for 35% of the time, Pallas kernels for 0%

commit v1 on v0

v1 whole, which is shorter than its diff:
```python
import math

import jax
import jax.numpy as jnp
import numpy as np
from jax import lax
from jax.experimental import pallas as pl
from jax.experimental.pallas import tpu as pltpu
from jax.sharding import PartitionSpec as P

MESH = pl.DeviceIdType.MESH
M = 16
NP = 8
CH = 2
courant = 1.0 / 6.0
time_step = 0.25
rate_scale = 0.25
f32 = jnp.float32
bf16 = jnp.bfloat16


def times_root(re, im, k, n, sign):
    k = k % n
    if k == 0:
        return re, im
    if 4 * k == n:
        return (-im, re) if sign > 0 else (im, -re)
    if 2 * k == n:
        return -re, -im
    if 4 * k == 3 * n:
        return (im, -re) if sign > 0 else (-im, re)
    c, s = math.cos(2 * math.pi * k / n), sign * math.sin(2 * math.pi * k / n)
    if 8 * k % n == 0:
        r = math.sqrt(0.5)
        cs, ss = (1 if c > 0 else -1), (1 if s > 0 else -1)
        a = re if cs > 0 else -re
        b = im if ss > 0 else -im
        d = re if ss > 0 else -re
        e = im if cs > 0 else -im
        return (a - b) * r, (d + e) * r
    return re * c - im * s, re * s + im * c


def transform(values, sign):
    n = len(values)
    if n == 1:
        return values
    even = transform(values[0::2], sign)
    odd = transform(values[1::2], sign)
    out = [None] * n
    for k in range(n // 2):
        tr, ti = times_root(*odd[k], k, n, sign)
        er, ei = even[k]
        out[k] = (er + tr, ei + ti)
        out[k + n // 2] = (er - tr, ei - ti)
    return out


def real_transform(values):
    n = len(values)
    if n == 1:
        return [(values[0], None)]
    if n == 2:
        return [(values[0] + values[1], None), (values[0] - values[1], None)]
    even = real_transform(values[0::2])
    odd = real_transform(values[1::2])
    out = [None] * (n // 2 + 1)
    h = n // 2
    for k in range(n // 4 + 1):
        er, ei = even[k]
        o_r, o_i = odd[k]
        if k == 0:
            out[0] = (er + o_r, None)
            out[h] = (er - o_r, None)
        elif k == n // 4:
            out[k] = (er, -o_r)
        else:
            tr, ti = times_root(o_r, o_i, k, n, -1)
            out[k] = (er + tr, ei + ti)
            out[h - k] = (er - tr, ti - ei)
    return out


def minmod(p, q):
    return jnp.minimum(jnp.maximum(p, jnp.minimum(q, 0.0)), jnp.maximum(q, 0.0))


def turned(v, by):
    n = v.shape[-2]
    if by > 0:
        return jnp.concatenate([v[..., n - 1 :, :], v[..., : n - 1, :]], axis=-2)
    return jnp.concatenate([v[..., 1:, :], v[..., :1, :]], axis=-2)


def moved(g, low, high, positive, vel_x, vel_y, vel_z, zs):
    sign = 0.5 if positive else -0.5
    here = g[zs[0] : zs[-1] + 1]
    planes = jnp.concatenate([low, here, high], axis=1)
    d = planes[:, 1:] - planes[:, :-1]
    face = planes[:, 1:4] + sign * minmod(d[:, :-1], d[:, 1:])
    jump_x = face[:, 1:] - face[:, :-1]

    up_y = vel_y > 0.0
    half_y = jnp.where(up_y, 0.5, -0.5)
    d = here - turned(here, 1)
    face = here + half_y * minmod(d, turned(d, -1))
    e = face - turned(face, 1)
    jump_y = jnp.where(up_y, e, turned(e, -1))

    up_z = vel_z > 0.0
    half_z = jnp.where(up_z, 0.5, -0.5)
    d = [g[z] - g[(z + 3) % 4] for z in range(4)]
    face = [g[z] + half_z * minmod(d[z], d[(z + 1) % 4]) for z in range(4)]
    e = [face[z] - face[(z + 3) % 4] for z in range(4)]
    jump_z = jnp.stack([jnp.where(up_z, e[z], e[(z + 1) % 4]) for z in zs])
    return here - courant * (vel_x * jump_x + vel_y * jump_y + vel_z * jump_z)


def lane_velocities(c_hi):
    lane = lax.broadcasted_iota(jnp.int32, (1, 128), 1)
    vel_x = (2.0 * ((lane >> 4) + 8 * c_hi).astype(f32) + 1.0) / M - 1.0
    vel_y = (2.0 * (lane & 15).astype(f32) + 1.0) / M - 1.0
    return vel_x, vel_y


def level(a):
    return (2.0 * a.astype(f32) + 1.0) / M - 1.0


def split(v):
    hi = v.astype(bf16)
    lo = (v - hi.astype(f32)).astype(bf16)
    return hi, lo


def product(v, weights):
    hi, lo = split(v)
    return jnp.dot(
        jnp.concatenate([hi, lo, hi], axis=1), weights, preferred_element_type=f32
    )


def wide(v):
    return jnp.concatenate([v[0], v[1]], axis=1)


def relaxed_cells(k, x_ref, tables, w_forward, w_inverse, spec, gain, out_ref):
    rows = [wide(x_ref[k, a]) * (1.0 / M**3) for a in range(M)]
    modes = real_transform(rows)
    parts = [re for re, _ in modes] + [im for _, im in modes[1:8]]
    both = product(jnp.concatenate(parts, axis=0), w_forward[...])
    both = [both[8 * i : 8 * i + 8] for i in range(16)]
    for q in range(9):
        rc, rs = both[q][:, :256], both[q][:, 256:]
        if q in (0, 8):
            spec[q, 0] = rc
            spec[q, 1] = -rs
            continue
        ic, js = both[q + 8][:, :256], both[q + 8][:, 256:]
        spec[q, 0] = rc + js
        spec[q, 1] = ic - rs
        spec[16 - q, 0] = rc - js
        spec[16 - q, 1] = -ic - rs

    def bent(m):
        values = []
        for q in range(M):
            t = tables[m, q]
            values.append((t * spec[q, 0], t * spec[q, 1]))
        values = transform(values, 1)
        return jnp.concatenate(
            [jnp.concatenate([re, im], axis=1) for re, im in values], axis=0
        )

    loss = product(bent(8), w_inverse[:, :256])
    gain[...] = -(jnp.concatenate([wide(x_ref[k, a]) for a in range(M)], axis=0) * loss)

    def term(p, c):
        both = product(jnp.concatenate([bent(p), bent(p + 4)], axis=0), w_inverse[...])
        left, right = both[:128], both[128:]
        gain[...] += left[:, :256] * right[:, :256] - left[:, 256:] * right[:, 256:]
        return c

    lax.fori_loop(0, 4, term, 0)

    velocities = [lane_velocities(c) for c in range(2)]
    weight = (2.0 / M) ** 3
    vz = [(2.0 * a + 1.0) / M - 1.0 for a in range(M)]
    cells = [x_ref[k, a] for a in range(M)]
    s0 = sum(cells[1:], cells[0])
    s1 = sum((cells[a] * vz[a] for a in range(1, M)), cells[0] * vz[0])
    s2 = sum((cells[a] * (vz[a] * vz[a]) for a in range(1, M)), cells[0] * (vz[0] * vz[0]))

    def total(v):
        return jnp.sum(v, axis=-1, keepdims=True) * weight

    (vx0, vy0), (vx1, vy1) = velocities
    mass = total(s0[0] + s0[1])
    mean_x = total(s0[0] * vx0 + s0[1] * vx1) / mass
    mean_y = total(s0[0] * vy0 + s0[1] * vy1) / mass
    mean_z = total(s1[0] + s1[1]) / mass
    energy = (
        total(
            s0[0] * (vx0 * vx0 + vy0 * vy0) + s0[1] * (vx1 * vx1 + vy1 * vy1) + s2[0] + s2[1]
        )
        / mass
    )
    heat = (energy - (mean_x * mean_x + mean_y * mean_y + mean_z * mean_z)) / 3.0
    variance = 2.0 * math.pi * heat
    rate = rate_scale * mass
    scale = time_step * rate * mass / (variance * jnp.sqrt(variance))
    inverse_heat = -1.0 / (2.0 * heat)
    divisor = 1.0 / (1.0 + time_step * rate)
    flat = [(vx - mean_x) ** 2 + (vy - mean_y) ** 2 for vx, vy in velocities]
    for a in range(M):
        away = (vz[a] - mean_z) ** 2
        for c in range(2):
            maxwell = scale * jnp.exp((flat[c] + away) * inverse_heat)
            change = gain[8 * a : 8 * a + 8, 128 * c : 128 * c + 128]
            out_ref[k, a, c] = (x_ref[k, a, c] + time_step * change + maxwell) * divisor


def kernel(
    g,
    gl,
    gr,
    lk,
    w_forward,
    w_inverse,
    out,
    halo_a,
    halo_b,
    adv,
    cells,
    ready,
    field,
    tables,
    spec,
    gain,
    halo_send,
    halo_recv,
    out_send,
    out_recv,
    back_send,
    back_recv,
    local_sem,
):
    s = lax.axis_index("space")
    j = lax.axis_index("vel")
    count = lax.axis_size("space")
    after = (lax.rem(s + 1, count), j)
    before = (lax.rem(s + count - 1, count), j)
    peers = [lax.rem(j + o, NP) for o in range(NP)]

    barrier = pltpu.get_barrier_semaphore()
    for d in (after, before):
        pl.semaphore_signal(barrier, inc=1, device_id=d, device_id_type=MESH)
    for o in range(1, NP):
        pl.semaphore_signal(barrier, inc=1, device_id=(s, peers[o]), device_id_type=MESH)

    for p in range(4):
        for q in range(M):
            tables[p, q] = jnp.broadcast_to(gl[p : p + 1, 256 * q : 256 * q + 256], (8, 256))
            tables[p + 4, q] = jnp.broadcast_to(gr[p : p + 1, 256 * q : 256 * q + 256], (8, 256))
    for q in range(M):
        tables[8, q] = jnp.broadcast_to(lk[0:1, 256 * q : 256 * q + 256], (8, 256))

    pl.semaphore_wait(barrier, NP + 1)

    def halo_copies(step, source, landing, k):
        low_two, low_one, high_two, high_one = landing
        zs = pl.ds(2 * k, 2)
        pairs = (
            (source.at[zs, :, 1], low_two.at[zs], after),
            (source.at[zs, :, 0, 1], low_one.at[zs], after),
            (source.at[zs, :, 0], high_two.at[zs], before),
            (source.at[zs, :, 1, 0], high_one.at[zs], before),
        )
        return [
            pltpu.make_async_remote_copy(
                src_ref=src,
                dst_ref=dst,
                send_sem=halo_send.at[step, k, i],
                recv_sem=halo_recv.at[step, k, i],
                device_id=d,
                device_id_type=MESH,
            )
            for i, (src, dst, d) in enumerate(pairs)
        ]

    def planes_beside(landing, a_l, c_hi, zs):
        low_two, low_one, high_two, high_one = landing
        if c_hi:
            return low_two[zs, a_l], high_one[zs, a_l][:, None]
        return low_one[zs, a_l][:, None], high_two[zs, a_l]

    def out_copy(k, o):
        return pltpu.make_async_remote_copy(
            src_ref=adv.at[k, peers[o]],
            dst_ref=cells.at[k, pl.ds(2 * j, 2)],
            send_sem=out_send.at[k, o],
            recv_sem=out_recv.at[k, o],
            device_id=(s, peers[o]),
            device_id_type=MESH,
        )

    def place(k, owner):
        return field.at[
            2 * k + lax.rem(lax.div(owner, 2), 2),
            :,
            :,
            lax.div(owner, 4),
            pl.ds(pl.multiple_of(8 * lax.rem(owner, 2), 8), 8),
        ]

    def back_copy(k, o):
        return pltpu.make_async_remote_copy(
            src_ref=ready.at[k, pl.ds(2 * peers[o], 2)],
            dst_ref=place(k, j),
            send_sem=back_send.at[k, o],
            recv_sem=back_recv.at[k, o],
            device_id=(s, peers[o]),
            device_id_type=MESH,
        )

    first = [halo_copies(0, g, halo_a, k) for k in range(CH)]
    for copies in first:
        for copy in copies:
            copy.start()

    outs = [[out_copy(k, o) for o in range(1, NP)] for k in range(CH)]
    own_out = [
        pltpu.make_async_copy(adv.at[k, j], cells.at[k, pl.ds(2 * j, 2)], local_sem.at[0, k])
        for k in range(CH)
    ]
    for k in range(CH):
        for copy in first[k]:
            copy.wait_recv()

        def advance(a_l, c):
            vel_z = jnp.full((1, 128), level(2 * j + a_l), f32)
            for c_hi in range(2):
                vel_x, vel_y = lane_velocities(c_hi)
                low, high = planes_beside(halo_a, a_l, c_hi, pl.ds(2 * k, 2))
                new = moved(
                    g[:, a_l, c_hi], low, high, c_hi == 1, vel_x, vel_y, vel_z, (2 * k, 2 * k + 1)
                )
                for x in range(2):
                    for z in range(2):
                        for h in range(2):
                            adv[k, 4 * x + 2 * z + h, a_l, c_hi] = new[z, x, 8 * h : 8 * h + 8]
            return c

        lax.fori_loop(0, 2, advance, 0)
        for copy in outs[k]:
            copy.start()
        own_out[k].start()

    backs = [[back_copy(k, o) for o in range(1, NP)] for k in range(CH)]
    own_back = [
        pltpu.make_async_copy(ready.at[k, pl.ds(2 * j, 2)], place(k, j), local_sem.at[1, k])
        for k in range(CH)
    ]
    for k in range(CH):
        own_out[k].wait()
        for copy in outs[k]:
            copy.wait_recv()
        relaxed_cells(k, cells, tables, w_forward, w_inverse, spec, gain, ready)
        for copy in backs[k]:
            copy.start()
        own_back[k].start()

    second = [halo_copies(1, field, halo_b, k) for k in range(CH)]
    for k in range(CH):
        own_back[k].wait()
        for copy in backs[k]:
            copy.wait_recv()
        for copy in second[k]:
            copy.start()
    for k in range(CH):
        for copy in second[k]:
            copy.wait_recv()

    def finish(a_l, c):
        vel_z = jnp.full((1, 128), level(2 * j + a_l), f32)
        for c_hi in range(2):
            vel_x, vel_y = lane_velocities(c_hi)
            low, high = planes_beside(halo_b, a_l, c_hi, pl.ds(0, 4))
            out[:, a_l, c_hi] = moved(
                field[:, a_l, c_hi], low, high, c_hi == 1, vel_x, vel_y, vel_z, (0, 1, 2, 3)
            )
        return c

    lax.fori_loop(0, 2, finish, 0)
    for group in (*first, *second, *outs, *backs):
        for copy in group:
            copy.wait_send()


def weights():
    index = np.arange(256)
    phase = (index[:, None] // 16 * (index[None, :] // 16) + index[:, None] % 16 * (index[None, :] % 16)) % 16
    cos, sin = np.cos(phase * (np.pi / 8)), np.sin(phase * (np.pi / 8))

    def held(m):
        m = m.astype(np.float32)
        hi = m.astype(jnp.bfloat16)
        lo = (m - hi.astype(np.float32)).astype(jnp.bfloat16)
        return np.concatenate([hi, hi, lo], axis=0)

    forward = held(np.concatenate([cos, sin], axis=1))
    inverse = held(np.block([[cos, sin], [-sin, cos]]))
    return forward, inverse


def per_device(density, gain_left, gain_right, loss_kernel):
    forward, inverse = weights()
    g = density.reshape(2, 16, 4, 2, 2, 128).transpose(2, 3, 4, 0, 1, 5)
    vmem = pl.BlockSpec(memory_space=pltpu.VMEM)
    dma = pltpu.SemaphoreType.DMA
    landing = (
        pltpu.VMEM((4, 2, 2, 16, 128), f32),
        pltpu.VMEM((4, 2, 16, 128), f32),
        pltpu.VMEM((4, 2, 2, 16, 128), f32),
        pltpu.VMEM((4, 2, 16, 128), f32),
    )
    new = pl.pallas_call(
        kernel,
        out_shape=jax.ShapeDtypeStruct(g.shape, f32),
        in_specs=[vmem] * 6,
        out_specs=vmem,
        scratch_shapes=[
            landing,
            landing,
            pltpu.VMEM((CH, NP, 2, 2, 8, 128), f32),
            pltpu.VMEM((CH, M, 2, 8, 128), f32),
            pltpu.VMEM((CH, M, 2, 8, 128), f32),
            pltpu.VMEM(g.shape, f32),
            pltpu.VMEM((9, M, 8, 256), f32),
            pltpu.VMEM((M, 2, 8, 256), f32),
            pltpu.VMEM((128, 256), f32),
            dma((2, CH, 4)),
            dma((2, CH, 4)),
            dma((CH, NP)),
            dma((CH, NP)),
            dma((CH, NP)),
            dma((CH, NP)),
            dma((2, CH)),
        ],
        compiler_params=pltpu.CompilerParams(
            collective_id=0, has_side_effects=True, vmem_limit_bytes=48 * 1024 * 1024
        ),
    )(g, gain_left, gain_right, loss_kernel.reshape(1, -1), jnp.asarray(forward), jnp.asarray(inverse))
    return new.transpose(3, 4, 0, 1, 2, 5).reshape(density.shape)


def solution(mesh):
    in_specs = (P("space", None, None, "vel"), P(), P(), P())
    out_specs = P("space", None, None, "vel")
    return jax.shard_map(
        per_device, mesh=mesh, in_specs=in_specs, out_specs=out_specs, check_vma=False
    )
```

time: 228 us -> 81.2 us (0.36)
  the two profiles are of different devices: /device:TPU:32 before, /device:TPU:64 now
where the time goes in v1:
time: 81.2 us; the launch traced here: 80.9 us
  Pallas kernels  74.6 us (92%)
  local copies, waits for them, and re-layouts  6.3 us (8%)
    pallas_call x1, Pallas kernels, per_device(): pl.pallas_call(kernel, out_shape=jax.ShapeDtypeStruct(g.shape, f32), in_s...  74.6 us
    unnamed x10, local copies, waits for them, and re-layouts  3.8 us

profile of v1, /device:TPU:64, one launch (start us, length us, event | category | flops | bytes accessed | tf_op | source)
XLA Modules:
  0.0 80.9 jit_solution(15043288357289520552)
XLA Ops:
  0.0 0.0 copy-start.1
  0.0 1.2 %reshape.12 = f32[2,16,4,2,2,128]{5,4,3,2,1,0:T(2,128)S(1)} reshape(f32[2,16,4,512]{3,2,1,0:T(4,128)} %param.6) | data formatting | bytes 524288 | tf_op jit(solution)/shard_map/reshape | solution.py:418
  1.3 0.1 copy.16
  1.3 0.0 copy-done.1
  1.4 0.0 copy-start
  1.4 1.4 %copy-done = bf16[1536,512]{1,0:T(8,128)(2,1)S(1)} copy-done((bf16[1536,512]{1,0:T(8,128)(2,1)S(1)}, bf16[1536,512]{1,0:T(8,128)(2,1)}, u32[]{:S(2)}) %copy-start) | copy-done | bytes 1572888
  2.8 0.0 copy-start.2
  2.8 0.8 %copy-done.2 = f32[4,4096]{1,0:T(4,128)S(1)} copy-done((f32[4,4096]{1,0:T(4,128)S(1)}, f32[4,4096]{1,0:T(4,128)}, u32[]{:S(2)}) %copy-start.2) | copy-done | bytes 65560
  3.6 0.0 copy-start.3
  3.6 0.8 %copy-done.3 = f32[4,4096]{1,0:T(4,128)S(1)} copy-done((f32[4,4096]{1,0:T(4,128)S(1)}, f32[4,4096]{1,0:T(4,128)}, u32[]{:S(2)}) %copy-start.3) | copy-done | bytes 65560
  4.5 0.0 copy-start.4
  4.5 0.7 copy-done.4
  5.2 74.6 %shard_map.64 = f32[4,2,2,2,16,128]{5,4,3,2,1,0:T(8,128)S(1)} custom-call(f32[4,2,2,2,16,128]{5,4,3,2,1,0:T(8,128)S(1)} %bitcast.5, f32[4,4096]{1,0:T(4,128)S(1)} %copy-done.2, f32[4,4096]{1,0:T(4,128)S(1)} %copy-done.3, f32[1,4096]{1,0:T(1,128)S(1)} %bitcast.7, bf16[768,512]{1,0:T(8,128)(2,1)S(1)} %copy-done.1, bf16[1536,512]{1,0:T(8,128)(2,1)S(1)} %copy-done), custom_call_target="tpu_custom_call" | custom-call | tf_op jit(solution)/shard_map/pallas_call | solution.py:427
  79.8 0.2 copy.13
  80.0 1.0 %reshape.13 = f32[2,16,4,512]{3,2,1,0:T(4,128)} reshape(f32[2,16,4,2,2,128]{5,4,3,2,1,0:T(2,128)S(1)} %copy.13) | data formatting | bytes 524288 | tf_op jit(solution)/shard_map/reshape | solution.py:454
Async XLA Ops:
  0.0 1.4 %copy-start.1 = (bf16[768,512]{1,0:T(8,128)(2,1)S(1)}, bf16[768,512]{1,0:T(8,128)(2,1)}, u32[]{:S(2)}) copy-start(bf16[768,512]{1,0:T(8,128)(2,1)} %constant.4.clone.w_forward) | copy-start | bytes 2359300
  1.4 1.4 %copy-start = (bf16[1536,512]{1,0:T(8,128)(2,1)S(1)}, bf16[1536,512]{1,0:T(8,128)(2,1)}, u32[]{:S(2)}) copy-start(bf16[1536,512]{1,0:T(8,128)(2,1)} %constant.5.clone.w_inverse) | copy-start | bytes 4718596
  2.8 0.8 %copy-start.2 = (f32[4,4096]{1,0:T(4,128)S(1)}, f32[4,4096]{1,0:T(4,128)}, u32[]{:S(2)}) copy-start(f32[4,4096]{1,0:T(4,128)} %gl.1) | copy-start | bytes 196612
  3.6 0.8 %copy-start.3 = (f32[4,4096]{1,0:T(4,128)S(1)}, f32[4,4096]{1,0:T(4,128)}, u32[]{:S(2)}) copy-start(f32[4,4096]{1,0:T(4,128)} %gr.1) | copy-start | bytes 196612
  4.5 0.7 copy-start.4

commit v2 on v1

--- a/solution.py
+++ b/solution.py
@@ -11,6 +11,7 @@
 MESH = pl.DeviceIdType.MESH
 M = 16
 NP = 8
+RUN = 8
 CH = 2
 courant = 1.0 / 6.0
 time_step = 0.25
@@ -221,13 +222,20 @@
 
 
 def kernel(
-    g,
+    density,
+    gl_far,
+    gr_far,
+    lk_far,
+    w_forward_far,
+    w_inverse_far,
+    out,
+    raw,
     gl,
     gr,
     lk,
     w_forward,
     w_inverse,
-    out,
+    g,
     halo_a,
     halo_b,
     adv,
@@ -244,6 +252,10 @@
     back_send,
     back_recv,
     local_sem,
+    load_sem,
+    far_send,
+    far_recv,
+    ack,
 ):
     s = lax.axis_index("space")
     j = lax.axis_index("vel")
@@ -252,29 +264,64 @@
     before = (lax.rem(s + count - 1, count), j)
     peers = [lax.rem(j + o, NP) for o in range(NP)]
 
+    place_in_run = lax.rem(s, RUN)
+    is_first, is_last = place_in_run == 0, place_in_run == RUN - 1
+    is_edge = jnp.logical_or(is_first, is_last)
+    is_inner = jnp.logical_not(is_edge)
+    far_s = jnp.where(is_first, before[0], after[0])
+
     barrier = pltpu.get_barrier_semaphore()
-    for d in (after, before):
+
+    def tell(d):
         pl.semaphore_signal(barrier, inc=1, device_id=d, device_id_type=MESH)
+
+    @pl.when(is_edge)
+    def _():
+        for d in range(NP):
+            tell((far_s, d))
+
+    @pl.when(jnp.logical_and(is_inner, place_in_run != RUN - 2))
+    def _():
+        tell(after)
+
+    @pl.when(jnp.logical_and(is_inner, place_in_run != 1))
+    def _():
+        tell(before)
+
+    @pl.when(is_first)
+    def _():
+        tell(after)
+
+    @pl.when(is_last)
+    def _():
+        tell(before)
+
     for o in range(1, NP):
-        pl.semaphore_signal(barrier, inc=1, device_id=(s, peers[o]), device_id_type=MESH)
-
-    for p in range(4):
-        for q in range(M):
-            tables[p, q] = jnp.broadcast_to(gl[p : p + 1, 256 * q : 256 * q + 256], (8, 256))
-            tables[p + 4, q] = jnp.broadcast_to(gr[p : p + 1, 256 * q : 256 * q + 256], (8, 256))
-    for q in range(M):
-        tables[8, q] = jnp.broadcast_to(lk[0:1, 256 * q : 256 * q + 256], (8, 256))
-
-    pl.semaphore_wait(barrier, NP + 1)
-
+        tell((s, peers[o]))
+
+    loads = [
+        pltpu.make_async_copy(density, raw, load_sem.at[0]),
+        pltpu.make_async_copy(w_forward_far, w_forward, load_sem.at[1]),
+        pltpu.make_async_copy(w_inverse_far, w_inverse, load_sem.at[2]),
+        pltpu.make_async_copy(gl_far, gl, load_sem.at[3]),
+        pltpu.make_async_copy(gr_far, gr, load_sem.at[4]),
+        pltpu.make_async_copy(lk_far, lk, load_sem.at[5]),
+    ]
+    for load in loads:
+        load.start()
+    loads[0].wait()
+    for x in range(2):
+        for z in range(4):
+            for t in range(4):
+                g[z, t // 2, t % 2, x] = raw[x, :, z, 128 * t : 128 * t + 128]
     def halo_copies(step, source, landing, k):
-        low_two, low_one, high_two, high_one = landing
+        low, high = landing
         zs = pl.ds(2 * k, 2)
         pairs = (
-            (source.at[zs, :, 1], low_two.at[zs], after),
-            (source.at[zs, :, 0, 1], low_one.at[zs], after),
-            (source.at[zs, :, 0], high_two.at[zs], before),
-            (source.at[zs, :, 1, 0], high_one.at[zs], before),
+            (source.at[zs, :, 1], low.at[zs, :, 1], after),
+            (source.at[zs, :, 0, 1], low.at[zs, :, 0, 1], after),
+            (source.at[zs, :, 0], high.at[zs, :, 0], before),
+            (source.at[zs, :, 1, 0], high.at[zs, :, 1, 0], before),
         )
         return [
             pltpu.make_async_remote_copy(
@@ -289,10 +336,10 @@
         ]
 
     def planes_beside(landing, a_l, c_hi, zs):
-        low_two, low_one, high_two, high_one = landing
+        low, high = landing
         if c_hi:
-            return low_two[zs, a_l], high_one[zs, a_l][:, None]
-        return low_one[zs, a_l][:, None], high_two[zs, a_l]
+            return low[zs, a_l, 1], high[zs, a_l, 1, 0:1]
+        return low[zs, a_l, 0, 1:2], high[zs, a_l, 0]
 
     def out_copy(k, o):
         return pltpu.make_async_remote_copy(
@@ -323,10 +370,88 @@
             device_id_type=MESH,
         )
 
+    def far_copy(k, owner, d, sem, side, both):
+        low, high = halo_b
+        x = lax.div(owner, 4) if not isinstance(owner, int) else owner // 4
+        z = 2 * k + (lax.rem(lax.div(owner, 2), 2) if not isinstance(owner, int) else owner // 2 % 2)
+        odd = lax.rem(owner, 2) if not isinstance(owner, int) else owner % 2
+        ys = pl.ds(8 * odd if isinstance(owner, int) else pl.multiple_of(8 * odd, 8), 8)
+        there = low if side else high
+        if both:
+            src, dst = ready.at[k, 2 * d : 2 * d + 2], there.at[z, :, :, x, ys]
+        else:
+            src, dst = ready.at[k, 2 * d : 2 * d + 2, side], there.at[z, :, side, x, ys]
+        return pltpu.make_async_remote_copy(
+            src_ref=src,
+            dst_ref=dst,
+            send_sem=far_send.at[k, d],
+            recv_sem=far_recv.at[k, sem],
+            device_id=(far_s, d),
+            device_id_type=MESH,
+        )
+
+    def each_far(act, k):
+        for side, here in ((1, is_last), (0, is_first)):
+            for x in range(2):
+
+                @pl.when(jnp.logical_and(here, lax.div(j, 4) == x))
+                def _():
+                    for d in range(NP):
+                        act(far_copy(k, j, d, j, side, x == side))
+
+    def await_far(k):
+        for side, here in ((1, is_first), (0, is_last)):
+
+            @pl.when(here)
+            def _():
+                for owner in range(NP):
+                    far_copy(k, owner, 0, owner, side, owner // 4 == side).wait_recv()
+
     first = [halo_copies(0, g, halo_a, k) for k in range(CH)]
-    for copies in first:
+
+    def start(copies):
         for copy in copies:
             copy.start()
+
+    @pl.when(is_inner)
+    def _():
+        pl.semaphore_wait(barrier, NP + 1)
+
+    @pl.when(place_in_run == 1)
+    def _():
+        pl.semaphore_signal(ack, inc=1, device_id=before, device_id_type=MESH)
+
+    @pl.when(place_in_run == RUN - 2)
+    def _():
+        pl.semaphore_signal(ack, inc=1, device_id=after, device_id_type=MESH)
+
+    @pl.when(is_edge)
+    def _():
+        pl.semaphore_wait(ack, 1)
+
+    def start_near(copies):
+        pl.when(jnp.logical_not(is_last))(lambda: start(copies[:2]))
+        pl.when(jnp.logical_not(is_first))(lambda: start(copies[2:]))
+
+    for k in range(CH):
+        start_near(first[k])
+
+    @pl.when(is_edge)
+    def _():
+        pl.semaphore_wait(barrier, 2 * NP - 1)
+
+    for k in range(CH):
+        pl.when(is_last)(lambda k=k: start(first[k][:2]))
+        pl.when(is_first)(lambda k=k: start(first[k][2:]))
+
+    for load in loads[1:]:
+        load.wait()
+    for p in range(4):
+        for q in range(M):
+            tables[p, q] = jnp.broadcast_to(gl[p : p + 1, 256 * q : 256 * q + 256], (8, 256))
+            tables[p + 4, q] = jnp.broadcast_to(gr[p : p + 1, 256 * q : 256 * q + 256], (8, 256))
+    for q in range(M):
+        tables[8, q] = jnp.broadcast_to(lk[0:1, 256 * q : 256 * q + 256], (8, 256))
 
     outs = [[out_copy(k, o) for o in range(1, NP)] for k in range(CH)]
     own_out = [
@@ -366,6 +491,7 @@
         for copy in outs[k]:
             copy.wait_recv()
         relaxed_cells(k, cells, tables, w_forward, w_inverse, spec, gain, ready)
+        each_far(lambda copy: copy.start(), k)
         for copy in backs[k]:
             copy.start()
         own_back[k].start()
@@ -375,11 +501,11 @@
         own_back[k].wait()
         for copy in backs[k]:
             copy.wait_recv()
-        for copy in second[k]:
-            copy.start()
-    for k in range(CH):
-        for copy in second[k]:
-            copy.wait_recv()
+        start_near(second[k])
+    for k in range(CH):
+        pl.when(jnp.logical_not(is_first))(lambda k=k: [copy.wait_recv() for copy in second[k][:2]] and None)
+        pl.when(jnp.logical_not(is_last))(lambda k=k: [copy.wait_recv() for copy in second[k][2:]] and None)
+        await_far(k)
 
     def finish(a_l, c):
         vel_z = jnp.full((1, 128), level(2 * j + a_l), f32)
@@ -392,9 +518,13 @@
         return c
 
     lax.fori_loop(0, 2, finish, 0)
-    for group in (*first, *second, *outs, *backs):
+    for group in (*first, *outs, *backs):
         for copy in group:
             copy.wait_send()
+    for k in range(CH):
+        pl.when(jnp.logical_not(is_last))(lambda k=k: [copy.wait_send() for copy in second[k][:2]] and None)
+        pl.when(jnp.logical_not(is_first))(lambda k=k: [copy.wait_send() for copy in second[k][2:]] and None)
+        each_far(lambda copy: copy.wait_send(), k)
 
 
 def weights():
@@ -415,27 +545,30 @@
 
 def per_device(density, gain_left, gain_right, loss_kernel):
     forward, inverse = weights()
-    g = density.reshape(2, 16, 4, 2, 2, 128).transpose(2, 3, 4, 0, 1, 5)
+    held = (4, 2, 2, 2, 16, 128)
+    far = pl.BlockSpec(memory_space=pltpu.HBM)
     vmem = pl.BlockSpec(memory_space=pltpu.VMEM)
     dma = pltpu.SemaphoreType.DMA
-    landing = (
-        pltpu.VMEM((4, 2, 2, 16, 128), f32),
-        pltpu.VMEM((4, 2, 16, 128), f32),
-        pltpu.VMEM((4, 2, 2, 16, 128), f32),
-        pltpu.VMEM((4, 2, 16, 128), f32),
-    )
+    landing = (pltpu.VMEM(held, f32), pltpu.VMEM(held, f32))
     new = pl.pallas_call(
         kernel,
-        out_shape=jax.ShapeDtypeStruct(g.shape, f32),
-        in_specs=[vmem] * 6,
+        out_shape=jax.ShapeDtypeStruct(held, f32),
+        in_specs=[far] * 6,
         out_specs=vmem,
         scratch_shapes=[
+            pltpu.VMEM(density.shape, f32),
+            pltpu.VMEM(gain_left.shape, f32),
+            pltpu.VMEM(gain_right.shape, f32),
+            pltpu.VMEM((1, loss_kernel.shape[0]), f32),
+            pltpu.VMEM(forward.shape, bf16),
+            pltpu.VMEM(inverse.shape, bf16),
+            pltpu.VMEM(held, f32),
             landing,
             landing,
             pltpu.VMEM((CH, NP, 2, 2, 8, 128), f32),
             pltpu.VMEM((CH, M, 2, 8, 128), f32),
             pltpu.VMEM((CH, M, 2, 8, 128), f32),
-            pltpu.VMEM(g.shape, f32),
+            pltpu.VMEM(held, f32),
             pltpu.VMEM((9, M, 8, 256), f32),
             pltpu.VMEM((M, 2, 8, 256), f32),
             pltpu.VMEM((128, 256), f32),
@@ -446,11 +579,15 @@
             dma((CH, NP)),
             dma((CH, NP)),
             dma((2, CH)),
+            dma((6,)),
+            dma((CH, NP)),
+            dma((CH, NP)),
+            pltpu.SemaphoreType.REGULAR,
         ],
         compiler_params=pltpu.CompilerParams(
-            collective_id=0, has_side_effects=True, vmem_limit_bytes=48 * 1024 * 1024
+            collective_id=0, has_side_effects=True, vmem_limit_bytes=63 * 1024 * 1024
         ),
-    )(g, gain_left, gain_right, loss_kernel.reshape(1, -1), jnp.asarray(forward), jnp.asarray(inverse))
+    )(density, gain_left, gain_right, loss_kernel.reshape(1, -1), jnp.asarray(forward), jnp.asarray(inverse))
     return new.transpose(3, 4, 0, 1, 2, 5).reshape(density.shape)
 
 

time: 81.2 us -> 65.7 us (0.81)
  the two profiles are of different devices: /device:TPU:64 before, /device:TPU:1 now
where the time goes in v2:
time: 65.7 us; the launch traced here: 65.5 us
  Pallas kernels  63.4 us (96%)
  local copies, waits for them, and re-layouts  2.11 us (3%)
    pallas_call x1, Pallas kernels, per_device(): pl.pallas_call(kernel, out_shape=jax.ShapeDtypeStruct(held, f32), in_spec...  63.4 us
    reshape x2, local copies, waits for them, and re-layouts, per_device(): return new.transpose(3, 4, 0, 1, 2, 5).reshape(density.shape)  2.11 us

profile of v2, /device:TPU:1, one launch (start us, length us, event | category | flops | bytes accessed | tf_op | source)
XLA Modules:
  0.0 65.5 jit_solution(8763430636527275347)
XLA Ops:
  0.0 63.4 %shard_map.64 = f32[4,2,2,2,16,128]{5,4,3,2,1,0:T(8,128)} custom-call(f32[2,16,4,512]{3,2,1,0:T(4,128)} %density.1, f32[4,4096]{1,0:T(4,128)} %gl_far.1, f32[4,4096]{1,0:T(4,128)} %gr_far.1, f32[1,4096]{1,0:T(1,128)} %bitcast.3, bf16[768,512]{1,0:T(8,128)(2,1)} %constant.4.clone.w_forward_far, bf16[1536,512]{1,0:T(8,128)(2,1)} %constant.5.clone.w_inverse_far), custom_call_target="tpu_custom_call" | custom-call | tf_op jit(solution)/shard_map/pallas_call | solution.py:553
  63.4 1.2 %copy.9 = f32[2,16,4,2,2,128]{5,4,3,2,1,0:T(2,128)S(1)} copy(f32[2,16,4,2,2,128]{5,1,0,4,3,2:T(8,128)} %bitcast.2) | data formatting | bytes 524288 | tf_op jit(solution)/shard_map/reshape | solution.py:591
  64.6 1.0 %reshape.8 = f32[2,16,4,512]{3,2,1,0:T(4,128)} reshape(f32[2,16,4,2,2,128]{5,4,3,2,1,0:T(2,128)S(1)} %copy.9) | data formatting | bytes 524288 | tf_op jit(solution)/shard_map/reshape | solution.py:591

commit v3 on v2

--- a/solution.py
+++ b/solution.py
@@ -182,7 +182,8 @@
         gain[...] += left[:, :256] * right[:, :256] - left[:, 256:] * right[:, 256:]
         return c
 
-    lax.fori_loop(0, 4, term, 0)
+    for p in range(4):
+        term(p, 0)
 
     velocities = [lane_velocities(c) for c in range(2)]
     weight = (2.0 / M) ** 3
@@ -262,7 +263,13 @@
     count = lax.axis_size("space")
     after = (lax.rem(s + 1, count), j)
     before = (lax.rem(s + count - 1, count), j)
-    peers = [lax.rem(j + o, NP) for o in range(NP)]
+    order = [sorted((d for d in range(NP) if d != i), key=lambda d: -abs(d - i)) for i in range(NP)]
+    peers = []
+    for n in range(NP - 1):
+        d = jnp.int32(order[0][n])
+        for i in range(1, NP):
+            d = jnp.where(j == i, order[i][n], d)
+        peers.append(d)
 
     place_in_run = lax.rem(s, RUN)
     is_first, is_last = place_in_run == 0, place_in_run == RUN - 1
@@ -277,8 +284,7 @@
 
     @pl.when(is_edge)
     def _():
-        for d in range(NP):
-            tell((far_s, d))
+        tell((far_s, j))
 
     @pl.when(jnp.logical_and(is_inner, place_in_run != RUN - 2))
     def _():
@@ -296,8 +302,8 @@
     def _():
         tell(before)
 
-    for o in range(1, NP):
-        tell((s, peers[o]))
+    for d in peers:
+        tell((s, d))
 
     loads = [
         pltpu.make_async_copy(density, raw, load_sem.at[0]),
@@ -341,13 +347,23 @@
             return low[zs, a_l, 1], high[zs, a_l, 1, 0:1]
         return low[zs, a_l, 0, 1:2], high[zs, a_l, 0]
 
-    def out_copy(k, o):
+    def out_copy(k, d):
         return pltpu.make_async_remote_copy(
-            src_ref=adv.at[k, peers[o]],
+            src_ref=adv.at[k, d],
             dst_ref=cells.at[k, pl.ds(2 * j, 2)],
-            send_sem=out_send.at[k, o],
-            recv_sem=out_recv.at[k, o],
-            device_id=(s, peers[o]),
+            send_sem=out_send.at[k, d],
+            recv_sem=out_recv.at[k, j],
+            device_id=(s, d),
+            device_id_type=MESH,
+        )
+
+    def arrival(k, d, dst, sem):
+        return pltpu.make_async_remote_copy(
+            src_ref=adv.at[k, d],
+            dst_ref=dst,
+            send_sem=out_send.at[k, d],
+            recv_sem=sem.at[k, d],
+            device_id=(s, d),
             device_id_type=MESH,
         )
 
@@ -360,13 +376,13 @@
             pl.ds(pl.multiple_of(8 * lax.rem(owner, 2), 8), 8),
         ]
 
-    def back_copy(k, o):
+    def back_copy(k, d):
         return pltpu.make_async_remote_copy(
-            src_ref=ready.at[k, pl.ds(2 * peers[o], 2)],
+            src_ref=ready.at[k, pl.ds(2 * d, 2)],
             dst_ref=place(k, j),
-            send_sem=back_send.at[k, o],
-            recv_sem=back_recv.at[k, o],
-            device_id=(s, peers[o]),
+            send_sem=back_send.at[k, d],
+            recv_sem=back_recv.at[k, j],
+            device_id=(s, d),
             device_id_type=MESH,
         )
 
@@ -378,9 +394,9 @@
         ys = pl.ds(8 * odd if isinstance(owner, int) else pl.multiple_of(8 * odd, 8), 8)
         there = low if side else high
         if both:
-            src, dst = ready.at[k, 2 * d : 2 * d + 2], there.at[z, :, :, x, ys]
+            src, dst = ready.at[k, pl.ds(2 * d, 2)], there.at[z, :, :, x, ys]
         else:
-            src, dst = ready.at[k, 2 * d : 2 * d + 2, side], there.at[z, :, side, x, ys]
+            src, dst = ready.at[k, pl.ds(2 * d, 2), side], there.at[z, :, side, x, ys]
         return pltpu.make_async_remote_copy(
             src_ref=src,
             dst_ref=dst,
@@ -396,7 +412,7 @@
 
                 @pl.when(jnp.logical_and(here, lax.div(j, 4) == x))
                 def _():
-                    for d in range(NP):
+                    for d in (j, *reversed(peers)):
                         act(far_copy(k, j, d, j, side, x == side))
 
     def await_far(k):
@@ -438,12 +454,13 @@
 
     @pl.when(is_edge)
     def _():
-        pl.semaphore_wait(barrier, 2 * NP - 1)
-
-    for k in range(CH):
-        pl.when(is_last)(lambda k=k: start(first[k][:2]))
-        pl.when(is_first)(lambda k=k: start(first[k][2:]))
-
+        pl.semaphore_wait(barrier, NP)
+
+    def start_far(copies):
+        pl.when(is_last)(lambda: start(copies[:2]))
+        pl.when(is_first)(lambda: start(copies[2:]))
+
+    start_far(first[0])
     for load in loads[1:]:
         load.wait()
     for p in range(4):
@@ -452,8 +469,9 @@
             tables[p + 4, q] = jnp.broadcast_to(gr[p : p + 1, 256 * q : 256 * q + 256], (8, 256))
     for q in range(M):
         tables[8, q] = jnp.broadcast_to(lk[0:1, 256 * q : 256 * q + 256], (8, 256))
-
-    outs = [[out_copy(k, o) for o in range(1, NP)] for k in range(CH)]
+    start_far(first[1])
+
+    outs = [[out_copy(k, d) for d in peers] for k in range(CH)]
     own_out = [
         pltpu.make_async_copy(adv.at[k, j], cells.at[k, pl.ds(2 * j, 2)], local_sem.at[0, k])
         for k in range(CH)
@@ -481,15 +499,15 @@
             copy.start()
         own_out[k].start()
 
-    backs = [[back_copy(k, o) for o in range(1, NP)] for k in range(CH)]
+    backs = [[back_copy(k, d) for d in peers] for k in range(CH)]
     own_back = [
         pltpu.make_async_copy(ready.at[k, pl.ds(2 * j, 2)], place(k, j), local_sem.at[1, k])
         for k in range(CH)
     ]
     for k in range(CH):
         own_out[k].wait()
-        for copy in outs[k]:
-            copy.wait_recv()
+        for d in peers:
+            arrival(k, d, cells.at[k, pl.ds(2 * d, 2)], out_recv).wait_recv()
         relaxed_cells(k, cells, tables, w_forward, w_inverse, spec, gain, ready)
         each_far(lambda copy: copy.start(), k)
         for copy in backs[k]:
@@ -499,25 +517,29 @@
     second = [halo_copies(1, field, halo_b, k) for k in range(CH)]
     for k in range(CH):
         own_back[k].wait()
-        for copy in backs[k]:
-            copy.wait_recv()
+        for d in peers:
+            arrival(k, d, place(k, d), back_recv).wait_recv()
         start_near(second[k])
     for k in range(CH):
         pl.when(jnp.logical_not(is_first))(lambda k=k: [copy.wait_recv() for copy in second[k][:2]] and None)
         pl.when(jnp.logical_not(is_last))(lambda k=k: [copy.wait_recv() for copy in second[k][2:]] and None)
         await_far(k)
 
-    def finish(a_l, c):
+    def finish(a_l):
         vel_z = jnp.full((1, 128), level(2 * j + a_l), f32)
         for c_hi in range(2):
             vel_x, vel_y = lane_velocities(c_hi)
             low, high = planes_beside(halo_b, a_l, c_hi, pl.ds(0, 4))
-            out[:, a_l, c_hi] = moved(
+            new = moved(
                 field[:, a_l, c_hi], low, high, c_hi == 1, vel_x, vel_y, vel_z, (0, 1, 2, 3)
             )
-        return c
-
-    lax.fori_loop(0, 2, finish, 0)
+            lanes = slice(128 * (2 * a_l + c_hi), 128 * (2 * a_l + c_hi + 1))
+            for x in range(2):
+                for z in range(4):
+                    out[x, :, z, lanes] = new[z, x]
+
+    finish(0)
+    finish(1)
     for group in (*first, *outs, *backs):
         for copy in group:
             copy.wait_send()
@@ -550,9 +572,9 @@
     vmem = pl.BlockSpec(memory_space=pltpu.VMEM)
     dma = pltpu.SemaphoreType.DMA
     landing = (pltpu.VMEM(held, f32), pltpu.VMEM(held, f32))
-    new = pl.pallas_call(
+    return pl.pallas_call(
         kernel,
-        out_shape=jax.ShapeDtypeStruct(held, f32),
+        out_shape=jax.ShapeDtypeStruct(density.shape, f32),
         in_specs=[far] * 6,
         out_specs=vmem,
         scratch_shapes=[
@@ -588,7 +610,6 @@
             collective_id=0, has_side_effects=True, vmem_limit_bytes=63 * 1024 * 1024
         ),
     )(density, gain_left, gain_right, loss_kernel.reshape(1, -1), jnp.asarray(forward), jnp.asarray(inverse))
-    return new.transpose(3, 4, 0, 1, 2, 5).reshape(density.shape)
 
 
 def solution(mesh):

time: 65.7 us -> 64.2 us (0.977)
  the two profiles are of different devices: /device:TPU:1 before, /device:TPU:32 now
where the time goes in v3:
time: 64.2 us; the launch traced here: 64 us
  Pallas kernels  62.4 us (97%)
  local copies, waits for them, and re-layouts  1.67 us (3%)
    pallas_call x1, Pallas kernels, per_device(): pl.pallas_call(kernel, out_shape=jax.ShapeDtypeStruct(density.shape, f32)...  62.4 us
    unnamed x1, local copies, waits for them, and re-layouts  1.67 us

profile of v3, /device:TPU:32, one launch (start us, length us, event | category | flops | bytes accessed | tf_op | source)
XLA Modules:
  0.0 64.0 jit_solution(17434632878394093168)
XLA Ops:
  0.0 62.4 %shard_map.64 = f32[2,16,4,512]{3,2,1,0:T(4,128)} custom-call(f32[2,16,4,512]{3,2,1,0:T(4,128)} %density.1, f32[4,4096]{1,0:T(4,128)} %gl_far.1, f32[4,4096]{1,0:T(4,128)} %gr_far.1, f32[1,4096]{1,0:T(1,128)} %bitcast.1, bf16[768,512]{1,0:T(8,128)(2,1)} %constant.4.clone.w_forward_far, bf16[1536,512]{1,0:T(8,128)(2,1)} %constant.5.clone.w_inverse_far), custom_call_target="tpu_custom_call" | custom-call | tf_op jit(solution)/shard_map/pallas_call | solution.py:575
  62.4 1.7 %copy.8 = f32[2,16,4,512]{3,2,1,0:T(4,128)} copy(f32[2,16,4,512]{3,2,1,0:T(4,128)} %shard_map.64) | data formatting | bytes 524288

commit v4 on v3

--- a/solution.py
+++ b/solution.py
@@ -141,23 +141,32 @@
     )
 
 
-def wide(v):
-    return jnp.concatenate([v[0], v[1]], axis=1)
+def parted(v):
+    return jnp.concatenate([v[:, 16 * c : 16 * c + 16] for c in (*range(0, M, 2), *range(1, M, 2))], axis=1)
 
 
 def relaxed_cells(k, x_ref, tables, w_forward, w_inverse, spec, gain, out_ref):
-    rows = [wide(x_ref[k, a]) * (1.0 / M**3) for a in range(M)]
+    rows = [
+        jnp.concatenate([x_ref[k, a, 0] + x_ref[k, a, 1], x_ref[k, a, 0] - x_ref[k, a, 1]], axis=1)
+        * (1.0 / M**3)
+        for a in range(M)
+    ]
     modes = real_transform(rows)
     parts = [re for re, _ in modes] + [im for _, im in modes[1:8]]
-    both = product(jnp.concatenate(parts, axis=0), w_forward[...])
-    both = [both[8 * i : 8 * i + 8] for i in range(16)]
+    parts = jnp.concatenate(parts, axis=0)
+    both = [product(parts[:, 128 * r : 128 * r + 128], w_forward[r]) for r in range(2)]
+    cosines, sines = (
+        jnp.concatenate([part[:, 128 * i : 128 * i + 128] for part in both], axis=1) for i in range(2)
+    )
+    cosines = [cosines[8 * i : 8 * i + 8] for i in range(16)]
+    sines = [sines[8 * i : 8 * i + 8] for i in range(16)]
     for q in range(9):
-        rc, rs = both[q][:, :256], both[q][:, 256:]
+        rc, rs = cosines[q], sines[q]
         if q in (0, 8):
             spec[q, 0] = rc
             spec[q, 1] = -rs
             continue
-        ic, js = both[q + 8][:, :256], both[q + 8][:, 256:]
+        ic, js = cosines[q + 8], sines[q + 8]
         spec[q, 0] = rc + js
         spec[q, 1] = ic - rs
         spec[16 - q, 0] = rc - js
@@ -169,21 +178,34 @@
             t = tables[m, q]
             values.append((t * spec[q, 0], t * spec[q, 1]))
         values = transform(values, 1)
-        return jnp.concatenate(
-            [jnp.concatenate([re, im], axis=1) for re, im in values], axis=0
-        )
-
-    loss = product(bent(8), w_inverse[:, :256])
-    gain[...] = -(jnp.concatenate([wide(x_ref[k, a]) for a in range(M)], axis=0) * loss)
-
-    def term(p, c):
-        both = product(jnp.concatenate([bent(p), bent(p + 4)], axis=0), w_inverse[...])
-        left, right = both[:128], both[128:]
-        gain[...] += left[:, :256] * right[:, :256] - left[:, 256:] * right[:, 256:]
-        return c
+        return [
+            jnp.concatenate(
+                [
+                    jnp.concatenate([v[:, 128 * r : 128 * r + 128] for v in pair], axis=1)
+                    for pair in values
+                ],
+                axis=0,
+            )
+            for r in range(2)
+        ]
+
+    loss = [product(half, w_inverse[r, :, :128]) for r, half in enumerate(bent(8))]
+    for c in range(2):
+        held = jnp.concatenate([x_ref[k, a, c] for a in range(M)], axis=0)
+        total_loss = loss[0] + loss[1] if c == 0 else loss[0] - loss[1]
+        gain[:, 128 * c : 128 * c + 128] = -(held * total_loss)
 
     for p in range(4):
-        term(p, 0)
+        halves = [
+            product(jnp.concatenate([left, right], axis=0), w_inverse[r])
+            for r, (left, right) in enumerate(zip(bent(p), bent(p + 4)))
+        ]
+        for c in range(2):
+            both = halves[0] + halves[1] if c == 0 else halves[0] - halves[1]
+            left, right = both[:128], both[128:]
+            gain[:, 128 * c : 128 * c + 128] += (
+                left[:, :128] * right[:, :128] - left[:, 128:] * right[:, 128:]
+            )
 
     velocities = [lane_velocities(c) for c in range(2)]
     weight = (2.0 / M) ** 3
@@ -463,12 +485,13 @@
     start_far(first[0])
     for load in loads[1:]:
         load.wait()
-    for p in range(4):
-        for q in range(M):
-            tables[p, q] = jnp.broadcast_to(gl[p : p + 1, 256 * q : 256 * q + 256], (8, 256))
-            tables[p + 4, q] = jnp.broadcast_to(gr[p : p + 1, 256 * q : 256 * q + 256], (8, 256))
     for q in range(M):
-        tables[8, q] = jnp.broadcast_to(lk[0:1, 256 * q : 256 * q + 256], (8, 256))
+        modes = slice(256 * q, 256 * q + 256)
+        lefts, rights, lost = parted(gl[:, modes]), parted(gr[:, modes]), parted(lk[:, modes])
+        for p in range(4):
+            tables[p, q] = jnp.broadcast_to(lefts[p : p + 1], (8, 256))
+            tables[p + 4, q] = jnp.broadcast_to(rights[p : p + 1], (8, 256))
+        tables[8, q] = jnp.broadcast_to(lost, (8, 256))
     start_far(first[1])
 
     outs = [[out_copy(k, d) for d in peers] for k in range(CH)]
@@ -550,9 +573,8 @@
 
 
 def weights():
-    index = np.arange(256)
-    phase = (index[:, None] // 16 * (index[None, :] // 16) + index[:, None] % 16 * (index[None, :] % 16)) % 16
-    cos, sin = np.cos(phase * (np.pi / 8)), np.sin(phase * (np.pi / 8))
+    index = np.arange(128)
+    forward, inverse = [], []
 
     def held(m):
         m = m.astype(np.float32)
@@ -560,9 +582,13 @@
         lo = (m - hi.astype(np.float32)).astype(jnp.bfloat16)
         return np.concatenate([hi, hi, lo], axis=0)
 
-    forward = held(np.concatenate([cos, sin], axis=1))
-    inverse = held(np.block([[cos, sin], [-sin, cos]]))
-    return forward, inverse
+    for r in range(2):
+        mode, speed = index[:, None], index[None, :]
+        phase = ((2 * (mode // 16) + r) * (speed // 16) + (mode % 16) * (speed % 16)) % 16
+        cos, sin = np.cos(phase * (np.pi / 8)), np.sin(phase * (np.pi / 8))
+        forward.append(held(np.concatenate([cos.T, sin.T], axis=1)))
+        inverse.append(held(np.block([[cos, sin], [-sin, cos]])))
+    return np.stack(forward), np.stack(inverse)
 
 
 def per_device(density, gain_left, gain_right, loss_kernel):

time: 64.2 us -> 63.3 us (0.986)
  Pallas kernels: 62.4 us -> 61.5 us
    pallas_call x1, Pallas kernels: 62.4 us -> 61.5 us  [per_device(): pl.pallas_call(kernel, out_shape=jax.ShapeDtypeStruct(density.shape, f32)...]
where the time goes in v4:
time: 63.3 us; the launch traced here: 63.2 us
  Pallas kernels  61.5 us (97%)
  local copies, waits for them, and re-layouts  1.67 us (3%)
    pallas_call x1, Pallas kernels, per_device(): pl.pallas_call(kernel, out_shape=jax.ShapeDtypeStruct(density.shape, f32)...  61.5 us
    unnamed x1, local copies, waits for them, and re-layouts  1.67 us

profile of v4, /device:TPU:32, one launch (start us, length us, event | category | flops | bytes accessed | tf_op | source)
XLA Modules:
  0.0 63.2 jit_solution(13178104075332039286)
XLA Ops:
  0.0 61.5 %shard_map.64 = f32[2,16,4,512]{3,2,1,0:T(4,128)} custom-call(f32[2,16,4,512]{3,2,1,0:T(4,128)} %density.1, f32[4,4096]{1,0:T(4,128)} %gl_far.1, f32[4,4096]{1,0:T(4,128)} %gr_far.1, f32[1,4096]{1,0:T(1,128)} %bitcast.1, bf16[2,384,256]{2,1,0:T(8,128)(2,1)} %constant.4.clone.w_forward_far, bf16[2,768,256]{2,1,0:T(8,128)(2,1)} %constant.5.clone.w_inverse_far), custom_call_target="tpu_custom_call" | custom-call | tf_op jit(solution)/shard_map/pallas_call | solution.py:601
  61.5 1.7 %copy.8 = f32[2,16,4,512]{3,2,1,0:T(4,128)} copy(f32[2,16,4,512]{3,2,1,0:T(4,128)} %shard_map.64) | data formatting | bytes 524288

commit v5 on v4

--- a/solution.py
+++ b/solution.py
@@ -279,6 +279,11 @@
     far_send,
     far_recv,
     ack,
+    passing_two,
+    passing_one,
+    pass_send,
+    pass_recv,
+    go,
 ):
     s = lax.axis_index("space")
     j = lax.axis_index("vel")
@@ -474,6 +479,53 @@
     for k in range(CH):
         start_near(first[k])
 
+    def handed(step):
+        zs = pl.ds(2, 2)
+        if step == 0:
+            ends = (
+                (g.at[zs, :, 1], passing_two, g.at[zs, :, 0, 1], passing_one, is_last, s - 2),
+                (g.at[zs, :, 0], passing_two, g.at[zs, :, 1, 0], passing_one, is_first, s + 2),
+            )
+        else:
+            low, high = halo_a
+            ends = (
+                (
+                    passing_two,
+                    low.at[zs, :, 1],
+                    passing_one,
+                    low.at[zs, :, 0, 1],
+                    place_in_run == RUN - 3,
+                    lax.rem(s + 3, count),
+                ),
+                (
+                    passing_two,
+                    high.at[zs, :, 0],
+                    passing_one,
+                    high.at[zs, :, 1, 0],
+                    place_in_run == 2,
+                    lax.rem(s + count - 3, count),
+                ),
+            )
+        found = []
+        for side, (two, two_to, one, one_to, here, to) in enumerate(ends):
+            copies = []
+            for i, (src, dst) in enumerate(((two, two_to), (one, one_to))):
+                copies.append(
+                    pltpu.make_async_remote_copy(
+                        src_ref=src,
+                        dst_ref=dst,
+                        send_sem=pass_send.at[step, i],
+                        recv_sem=pass_recv.at[i] if step == 0 else halo_recv.at[0, 1, 2 * side + i],
+                        device_id=(to, j),
+                        device_id_type=MESH,
+                    )
+                )
+            found.append((here, copies))
+        return found
+
+    for here, copies in handed(0):
+        pl.when(here)(lambda copies=copies: start(copies))
+
     @pl.when(is_edge)
     def _():
         pl.semaphore_wait(barrier, NP)
@@ -481,6 +533,14 @@
     def start_far(copies):
         pl.when(is_last)(lambda: start(copies[:2]))
         pl.when(is_first)(lambda: start(copies[2:]))
+
+    @pl.when(is_last)
+    def _():
+        pl.semaphore_signal(go, inc=1, device_id=(s - 2, j), device_id_type=MESH)
+
+    @pl.when(is_first)
+    def _():
+        pl.semaphore_signal(go, inc=1, device_id=(s + 2, j), device_id_type=MESH)
 
     start_far(first[0])
     for load in loads[1:]:
@@ -492,7 +552,17 @@
             tables[p, q] = jnp.broadcast_to(lefts[p : p + 1], (8, 256))
             tables[p + 4, q] = jnp.broadcast_to(rights[p : p + 1], (8, 256))
         tables[8, q] = jnp.broadcast_to(lost, (8, 256))
-    start_far(first[1])
+
+    for here, copies in handed(1):
+
+        @pl.when(here)
+        def _(copies=copies):
+            for copy in handed(0)[0][1]:
+                copy.wait_recv()
+            pl.semaphore_wait(go, 1)
+            start(copies)
+            for copy in copies:
+                copy.wait_send()
 
     outs = [[out_copy(k, d) for d in peers] for k in range(CH)]
     own_out = [
@@ -563,9 +633,16 @@
 
     finish(0)
     finish(1)
-    for group in (*first, *outs, *backs):
-        for copy in group:
+    def wait_sends(copies):
+        for copy in copies:
             copy.wait_send()
+
+    for group in (first[0], *outs, *backs):
+        wait_sends(group)
+    pl.when(jnp.logical_not(is_last))(lambda: wait_sends(first[1][:2]))
+    pl.when(jnp.logical_not(is_first))(lambda: wait_sends(first[1][2:]))
+    for here, copies in handed(0):
+        pl.when(here)(lambda copies=copies: wait_sends(copies))
     for k in range(CH):
         pl.when(jnp.logical_not(is_last))(lambda k=k: [copy.wait_send() for copy in second[k][:2]] and None)
         pl.when(jnp.logical_not(is_first))(lambda k=k: [copy.wait_send() for copy in second[k][2:]] and None)
@@ -631,6 +708,11 @@
             dma((CH, NP)),
             dma((CH, NP)),
             pltpu.SemaphoreType.REGULAR,
+            pltpu.VMEM((2, 2, 2, 16, 128), f32),
+            pltpu.VMEM((2, 2, 16, 128), f32),
+            dma((2, 2)),
+            dma((2,)),
+            pltpu.SemaphoreType.REGULAR,
         ],
         compiler_params=pltpu.CompilerParams(
             collective_id=0, has_side_effects=True, vmem_limit_bytes=63 * 1024 * 1024

time: 63.3 us -> 63.7 us (level)
  the two profiles are of different devices: /device:TPU:32 before, /device:TPU:1 now
where the time goes in v5:
time: 63.7 us; the launch traced here: 63.5 us
  Pallas kernels  61.9 us (97%)
  local copies, waits for them, and re-layouts  1.67 us (3%)
    pallas_call x1, Pallas kernels, per_device(): pl.pallas_call(kernel, out_shape=jax.ShapeDtypeStruct(density.shape, f32)...  61.9 us
    unnamed x1, local copies, waits for them, and re-layouts  1.67 us

profile of v5, /device:TPU:1, one launch (start us, length us, event | category | flops | bytes accessed | tf_op | source)
XLA Modules:
  0.0 63.5 jit_solution(2055447675676555988)
XLA Ops:
  0.0 61.9 %shard_map.64 = f32[2,16,4,512]{3,2,1,0:T(4,128)} custom-call(f32[2,16,4,512]{3,2,1,0:T(4,128)} %density.1, f32[4,4096]{1,0:T(4,128)} %gl_far.1, f32[4,4096]{1,0:T(4,128)} %gr_far.1, f32[1,4096]{1,0:T(1,128)} %bitcast.1, bf16[2,384,256]{2,1,0:T(8,128)(2,1)} %constant.4.clone.w_forward_far, bf16[2,768,256]{2,1,0:T(8,128)(2,1)} %constant.5.clone.w_inverse_far), custom_call_target="tpu_custom_call" | custom-call | tf_op jit(solution)/shard_map/pallas_call | solution.py:678
  61.9 1.7 %copy.8 = f32[2,16,4,512]{3,2,1,0:T(4,128)} copy(f32[2,16,4,512]{3,2,1,0:T(4,128)} %shard_map.64) | data formatting | bytes 524288
